TPU v7x, 1024 devices: a whole 4x4x32 slice. The times are simulated.
1024 devices in a mesh: replica: 16 (over z_lo), expert: 64 (over z_hi, y, x, core).
Axes of the slice: x: 4, y: 4, z: 32 (z_hi: 2, z_lo: 16; z = z_hi * 16 + z_lo), core: 2. Of those that a mesh axis runs over, the one named last changes fastest.
Arguments:
- tokens: bfloat16 [16, 8192, 2560], P('replica', 'expert'), may hold values from -6 to 6
- routes: int32 [16, 8192, 2], P('replica', 'expert'), may hold values from 0 to 63, all different within a row; in each aligned block of 128 rows (0 to 127, 128 to 255, ..., all dimensions but the last counted through in order) at most 6 rows name the same one
- route_weight: float32 [16, 8192, 2], P('replica', 'expert'), may hold values from 0.2 to 1
- gate_weight: bfloat16 [64, 2560, 768], P('expert'), may hold values from -0.125 to 0.125
- up_weight: bfloat16 [64, 2560, 768], P('expert'), may hold values from -0.125 to 0.125
- local_params: bfloat16 [16, 2048, 2048], P('replica', 'expert'), may hold values from -6 to 6
- base: float32 [2048, 2048], P('expert'), may hold values from -6 to 6
- momentum: float32 [2048, 2048], P('expert'), may hold values from -3 to 3
Outputs:
- mixed: bfloat16 [16, 8192, 2, 768], P('replica', 'expert')
- new_base: float32 [2048, 2048], P('expert')
- new_momentum: float32 [2048, 2048], P('expert')
Inputs may be any that keep to these rules, and one draw needn't show every extreme that they name: `routes`: the 2 experts of a token differ; the rows of one device name each expert at most 6 times, and some device names some expert exactly 6 times.
All inputs are finite; a program needn't handle non-finite values.
Results may differ from a plain program's by a relative error of at most 0.0049.
Values may be sent and summed in bfloat16 or wider, within the bound.
A program may use at most 32 MiB of HBM per device.

v0:
```python
import jax
import jax.numpy as jnp
from jax import lax
from jax.sharding import PartitionSpec as P

outer_rate = 0.7
outer_beta = 0.9


def shards(tokens, routes, route_weight, gate_weight, up_weight, local_params, base, momentum):
    rows = tokens[0]
    chosen = routes[0]
    weights = route_weight[0]
    count_dev = lax.axis_size("expert")
    tok_rows, topk = chosen.shape
    capacity = max(2, 3 * tok_rows * topk // (2 * count_dev))
    flat_pairs = chosen.reshape(-1)
    onehot = (flat_pairs[:, None] == jnp.arange(count_dev, dtype=jnp.int32)[None, :]).astype(
        jnp.int32
    )
    ranks = jnp.sum((jnp.cumsum(onehot, axis=0) - onehot) * onehot, axis=1)
    target = flat_pairs * capacity + ranks
    slot_ids = jnp.arange(count_dev * capacity, dtype=jnp.int32)
    picking = target[:, None] == slot_ids[None, :]
    placing = jnp.any(picking.reshape(tok_rows, topk, -1), axis=1).astype(jnp.bfloat16)
    outgoing = lax.dot_general(
        placing, rows, (((0,), (0,)), ((), ())), preferred_element_type=jnp.float32
    )
    outgoing = outgoing.astype(jnp.bfloat16).reshape(count_dev, capacity, rows.shape[1])
    w_gate = gate_weight[0]
    w_up = up_weight[0]
    received = lax.all_to_all(outgoing, "expert", split_axis=0, concat_axis=0, tiled=True)
    sources, slots, width = received.shape
    flat = received.reshape(sources * slots, width)
    gate = jnp.dot(flat, w_gate, preferred_element_type=jnp.float32)
    upper = jnp.dot(flat, w_up, preferred_element_type=jnp.float32)
    returned = lax.all_to_all(
        (jax.nn.silu(gate) * upper).astype(jnp.bfloat16).reshape(sources, slots, -1),
        "expert",
        split_axis=0,
        concat_axis=0,
        tiled=True,
    )
    collected = jnp.dot(
        picking.astype(jnp.bfloat16),
        returned.reshape(count_dev * capacity, -1),
        preferred_element_type=jnp.float32,
    )
    mixed = (weights.reshape(-1, 1) * collected).astype(jnp.bfloat16).reshape(1, tok_rows, topk, -1)
    n_replica = lax.axis_size("replica")
    delta = (base - local_params[0].astype(jnp.float32)).astype(jnp.bfloat16)
    delta = lax.optimization_barrier(delta).astype(jnp.float32)
    outer_grad = lax.psum(delta, "replica") / n_replica
    new_momentum = outer_beta * momentum + outer_grad
    new_base = base - outer_rate * (outer_grad + outer_beta * new_momentum)
    return (mixed, new_base, new_momentum)


def solution(mesh):
    in_specs = (
        P("replica", "expert", None),
        P("replica", "expert", None),
        P("replica", "expert", None),
        P("expert", None, None),
        P("expert", None, None),
        P("replica", "expert", None),
        P("expert", None),
        P("expert", None),
    )
    out_specs = (P("replica", "expert", None, None), P("expert", None), P("expert", None))
    return jax.shard_map(shards, mesh=mesh, in_specs=in_specs, out_specs=out_specs, check_vma=False)
```

profile of v0, /device:TPU:6, one launch (start us, length us, event | category | flops | bytes accessed | tf_op | source)
XLA Modules:
  0.0 519.4 jit_solution(16155293506146161180)
XLA Ops:
  0.6 0.0 copy-start
  0.6 0.9 copy.18
  1.5 0.1 eq.46
  1.6 0.1 reshape_squeeze.4
  1.8 0.6 reduce-window.6
  2.4 0.2 slice_reduce_fusion
  2.6 0.1 fusion.17
  2.7 0.1 reduce_sum.12
  2.9 0.1 copy.22
  3.0 0.1 fusion.12
  3.1 0.0 copy-done
  3.1 2.0 convolution_convert_fusion
  5.1 2.6 reshape.63
  7.7 132.3 %all_to_all.10 = bf16[64,6,2560]{2,1,0:T(8,128)(2,1)} all-to-all(bf16[64,6,2560]{2,1,0:T(8,128)(2,1)S(1)} %reshape.63), channel_id=1, replica_groups=mesh['replica'=16,'expert'=64] {'expert'}, dimensions={0} | all-to-all | bytes 3932160 | tf_op jit(solution)/shard_map/all_to_all | solution.py:32
  140.0 2.8 reshape.64
  142.8 0.0 copy-start.5
  142.8 3.9 fusion.2
  146.8 0.0 copy-done.5
  146.8 1.7 fusion.7
  148.5 0.0 copy-start.4
  148.5 0.0 copy-start.1
  148.6 0.0 copy-start.3
  148.6 0.0 copy-start.2
  148.6 1.1 reshape.65
  149.7 39.0 %all-to-all-start.1 = ((bf16[64,6,768]{2,1,0:T(8,128)(2,1)}), bf16[64,6,768]{2,1,0:T(8,128)(2,1)S(1)}, u32[]{:S(2)}, u32[]{:S(2)}) async-start(bf16[64,6,768]{2,1,0:T(8,128)(2,1)} %reshape.65), calls=%async_computation.1 | async-start | bytes 1572864 | tf_op jit(solution)/shard_map/all_to_all | solution.py:37
  188.7 0.0 copy-done.4
  188.7 0.1 copy.17
  188.8 0.1 mul.50
  189.0 0.0 copy-done.1
  189.0 0.0 copy-done.3
  189.0 328.0 %all-reduce.1 = f32[32,2048]{1,0:T(8,128)S(1)} all-reduce(bf16[32,2048]{1,0:T(8,128)(2,1)S(1)} %fusion.13), channel_id=1, replica_groups=mesh['replica'=16,'expert'=64] {'replica'}, use_global_device_ids=true, to_apply=%region_4.5 | all-reduce | flops 65536 | bytes 393216 | tf_op jit(solution)/shard_map/psum | solution.py:53
  517.0 0.0 copy-done.2
  517.0 0.9 multiply_subtract_fusion
  517.9 0.0 all-to-all-done.1
  517.9 0.2 reshape.66
  518.1 0.4 fusion.10
  518.5 0.9 reshape.67
  (6 shorter events, 0.1 us)
Async XLA Ops:
  0.6 2.5 copy-start
  142.8 4.0 copy-start.5
  148.5 40.2 %copy-start.4 = (f32[1,128,2]{1,2,0:T(2,128)S(1)}, f32[1,128,2]{1,2,0:T(2,128)}, u32[]{:S(2)}) copy-start(f32[1,128,2]{1,2,0:T(2,128)} %param.10) | copy-start | bytes 3076
  148.5 40.4 %copy-start.1 = (f32[32,2048]{1,0:T(8,128)S(1)}, f32[32,2048]{1,0:T(8,128)}, u32[]{:S(2)}) copy-start(f32[32,2048]{1,0:T(8,128)} %param.14) | copy-start | bytes 786436
  148.6 40.4 %copy-start.3 = (bf16[1,32,2048]{2,1,0:T(8,128)(2,1)S(1)}, bf16[1,32,2048]{2,1,0:T(8,128)(2,1)}, u32[]{:S(2)}) copy-start(bf16[1,32,2048]{2,1,0:T(8,128)(2,1)} %param.13) | copy-start | bytes 393220
  148.6 368.4 %copy-start.2 = (f32[32,2048]{1,0:T(8,128)S(1)}, f32[32,2048]{1,0:T(8,128)}, u32[]{:S(2)}) copy-start(f32[32,2048]{1,0:T(8,128)} %param.15) | copy-start | bytes 786436
  149.7 368.2 %all-to-all-start.1 = ((bf16[64,6,768]{2,1,0:T(8,128)(2,1)}), bf16[64,6,768]{2,1,0:T(8,128)(2,1)S(1)}, u32[]{:S(2)}, u32[]{:S(2)}) async-start(bf16[64,6,768]{2,1,0:T(8,128)(2,1)} %reshape.65), calls=%async_computation.1 | async-start | bytes 1572864 | tf_op jit(solution)/shard_map/all_to_all | solution.py:37
where the time goes:
time: 520 us; the launch traced here: 519 us
  blocking collectives  460 us (88%)
  starting transfers between devices  39 us (8%)
  local copies, waits for them, and re-layouts  9.35 us (2%)
  matrix products  8.11 us (2%)
    psum x1, blocking collectives, shards(): outer_grad = lax.psum(delta, 'replica') / n_replica  328 us
    all_to_all x1, blocking collectives, shards(): lax.all_to_all(outgoing, 'expert', split_axis=0, concat_axis=0, tiled=True)  132 us
    all_to_all x1, starting transfers between devices, shards(): lax.all_to_all((jax.nn.silu(gate) * upper).astype(jnp.bfloat16).reshape(s...  39 us
  transfers between devices with their start and end apart: 1, of which 0 were waited for; matrix products, arithmetic and copies ran while one was open for 0% of the time, Pallas kernels for 0%

commit v1 on v0

v1 whole, which is shorter than its diff:
```python
import jax
import jax.numpy as jnp
from jax import lax
from jax.experimental import pallas as pl
from jax.experimental.pallas import tpu as pltpu
from jax.sharding import PartitionSpec as P

MESH = pl.DeviceIdType.MESH
outer_rate = 0.7
outer_beta = 0.9

LINE = 16
PLANE = 32
ROWS = 16
TOK, DW, HW = 128, 2560, 768
CB = 256
NJ = HW // CB
CHUNK = 128
NR = DW // CHUNK
NB = 2 * NR
M = NJ * NB
SHIFT = 8
LEAD = 6
LAG = 45
PIECES = 4
CEN = 8
HOP = 3


def received(a):
    return M // 2 + ((LINE - 1 - 2 * a) * SHIFT) // 8


def kernel(tok, routes, weights, gate_hbm, up_hbm, local, base, mixed, total,
           own, oth, rel, outg, recvd, own_hid, hid, ret, pick, part, acc, xin,
           load_sem, recv_d, recv_r, fwd_d, fwd_r, x_s, own_r,
           disp_s, disp_r, ret_s, ret_r, loc_s, in_r, in_s, xin_r, xin_s, tot_r, tot_s):
    i = lax.axis_index("replica")
    e = lax.axis_index("expert")
    d = lax.rem(e, 2)
    half = e // PLANE
    me = lax.rem(e, PLANE)
    flip = lax.rem(e + PLANE, 2 * PLANE)
    mate = e + 1 - 2 * d
    mflip = lax.rem(mate + PLANE, 2 * PLANE)
    last = LINE - 1
    k = jnp.where(d == 0, i, last - i)
    end = jnp.where(d == 0, last, 0)
    way = 1 - 2 * d
    ni = lax.rem(i + way + LINE, LINE)
    pi = lax.rem(i - way + LINE, LINE)
    nxt = (ni, jnp.where(i == end, flip, e))
    prv = (pi, jnp.where(i == last - end, flip, e))
    opp = (pi, mflip)
    mid = (i, mate)

    def count(a):
        return jnp.where(d == 0, received(a), M - received(last - a))

    wopp = jnp.where(d == 0, M - received(last), received(0))

    def peer(n):
        q = lax.rem(me + 1 + n, PLANE)
        return q, (i, half * PLANE + q)

    barrier = pltpu.get_barrier_semaphore()
    for dev in (nxt, prv):
        pl.semaphore_signal(barrier, inc=1, device_id=dev, device_id_type=MESH)

    @pl.when(k == 0)
    def _():
        pl.semaphore_signal(barrier, inc=1, device_id=opp, device_id_type=MESH)

    loads = []
    for j in (0, *range(NJ - 1, 0, -1)):
        for g, ref in enumerate((gate_hbm, up_hbm)):
            loads.append(pltpu.make_async_copy(ref.at[:, pl.ds(j * CB, CB)], own.at[j, g], load_sem.at[j, g]))
    for copy in loads:
        copy.start()

    def greet(n, _):
        pl.semaphore_signal(barrier, inc=1, device_id=peer(n)[1], device_id_type=MESH)
        return 0

    lax.fori_loop(0, PLANE - 1, greet, 0)
    pl.semaphore_wait(barrier, PLANE + 1 + jnp.where(k == 0, 1, 0))
    for copy in loads:
        copy.wait()

    def at(buf, c):
        rows = pl.ds(pl.multiple_of(lax.rem(c, NB) // 2 * CHUNK, CHUNK), CHUNK)
        return buf.at[c // NB, lax.rem(c, 2), rows, :]

    def cp(src, dst, c, ss, rs, dev):
        return pltpu.make_async_remote_copy(src_ref=at(src, c), dst_ref=at(dst, c), send_sem=ss.at[c],
                                            recv_sem=rs.at[c], device_id=dev, device_id_type=MESH)

    def mine(s):
        return jnp.where(d == 0, s, M - 1 - s)

    def theirs(s):
        return jnp.where(d == 0, M - 1 - s, s)

    def opp_send(s):
        return cp(own, rel, theirs(s), own_r, recv_r, opp)

    def first_send(s):
        return cp(own, oth, mine(s), fwd_d, recv_d, nxt)

    def lead_body(s, _):
        pl.when(k == 0)(lambda: opp_send(s).start())
        pl.when(k == last)(lambda: first_send(s).start())
        return 0

    lax.fori_loop(0, LEAD, lead_body, 0)

    lanes = lax.broadcasted_iota(jnp.int32, (TOK, 2 * PLANE), 1)
    r = [routes[:, 0:1], routes[:, 1:2]]
    named = ((r[0] == lanes) | (r[1] == lanes)).astype(jnp.float32)
    before = (lax.broadcasted_iota(jnp.int32, (TOK, TOK), 1) < lax.broadcasted_iota(jnp.int32, (TOK, TOK), 0))
    ranks = jnp.dot(before.astype(jnp.bfloat16), named.astype(jnp.bfloat16), preferred_element_type=jnp.float32)
    slots = lax.broadcasted_iota(jnp.int32, (TOK, PLANE * ROWS), 1)
    place = jnp.zeros((TOK, PLANE * ROWS), jnp.float32)
    for t in range(2):
        rank = jnp.sum(jnp.where(r[t] == lanes, ranks, 0.0), axis=1, keepdims=True).astype(jnp.int32)
        row = (r[t] & (PLANE - 1)) * ROWS + jnp.where(r[t] // PLANE == half, 0, ROWS // 2) + rank
        one = (row == slots).astype(jnp.float32)
        pick[t] = one.astype(jnp.bfloat16)
        place += one
    place_t = place.T.astype(jnp.bfloat16)
    for c in range(DW // 512):
        cols = pl.ds(c * 512, 512)
        outg[:, cols] = jnp.dot(place_t, tok[:, cols], preferred_element_type=jnp.float32).astype(jnp.bfloat16)

    def block(q):
        return pl.ds(pl.multiple_of(q * ROWS, ROWS), ROWS)

    def dispatch(n):
        q, dev = peer(n)
        pltpu.make_async_remote_copy(src_ref=outg.at[block(q)], dst_ref=recvd.at[block(me)], send_sem=disp_s,
                                     recv_sem=disp_r, device_id=dev, device_id_type=MESH).start()

    own_rows = pltpu.make_async_copy(outg.at[block(me)], recvd.at[block(me)], loc_s.at[0])
    own_rows.start()

    @pl.when(k >= 8)
    def _():
        def body(n, _):
            dispatch(n)
            return 0
        lax.fori_loop(0, PLANE - 1, body, 0)

    width = part.shape[2]

    def pcopy(src, dst, c, ss, rs, dev):
        return pltpu.make_async_remote_copy(src_ref=src.at[c], dst_ref=dst.at[c], send_sem=ss.at[c],
                                            recv_sem=rs.at[c], device_id=dev, device_id_type=MESH)

    for c in range(PIECES):
        cols = pl.ds(c * width, width)
        delta = (base[:, cols] - local[:, cols].astype(jnp.float32)).astype(jnp.bfloat16)
        acc[c] = delta.astype(jnp.float32)

    @pl.when(k > CEN)
    def _():
        for c in range(PIECES):
            @pl.when(k < last)
            def _():
                pcopy(acc, part, c, in_s, in_r, prv).wait_recv()
                acc[c] = acc[c] + part[c]

            pl.when(k > CEN + 1)(lambda: pcopy(acc, part, c, in_s, in_r, prv).start())
            pl.when(k == CEN + 1)(lambda: pcopy(acc, xin, c, xin_s, xin_r, prv).start())

    def deltas(s):
        low = k <= CEN

        @pl.when(low & (s < PIECES))
        def _():
            @pl.when(k > 0)
            def _():
                pcopy(acc, part, s, in_s, in_r, nxt).wait_recv()
                acc[s] = acc[s] + part[s]

            pl.when(k < CEN)(lambda: pcopy(acc, part, s, in_s, in_r, nxt).start())
            pl.when(k == CEN)(lambda: pcopy(acc, xin, s, xin_s, xin_r, nxt).start())

        meet = s - jnp.where(low, 6, 1)

        @pl.when(((k == CEN) | (k == CEN + 1)) & (meet >= 0) & (meet < PIECES))
        def _():
            pcopy(acc, xin, meet, xin_s, xin_r, nxt).wait_recv()
            total[meet] = acc[meet] + xin[meet]
            pl.when(low)(lambda: pcopy(total, total, meet, tot_s, tot_r, prv).start())
            pl.when(k > CEN)(lambda: pcopy(total, total, meet, tot_s, tot_r, nxt).start())

        back = s - jnp.where(low, 2 * HOP * (CEN - k) + 6, 2)

        @pl.when(((k < CEN) | (k > CEN + 1)) & (back >= 0) & (back < PIECES))
        def _():
            pcopy(total, total, back, tot_s, tot_r, prv).wait_recv()
            pl.when((k < CEN) & (k > 0))(lambda: pcopy(total, total, back, tot_s, tot_r, prv).start())
            pl.when((k > CEN + 1) & (k < last))(lambda: pcopy(total, total, back, tot_s, tot_r, nxt).start())

    def gated(buf, j):
        g = jnp.dot(recvd[...], buf[j, 0], preferred_element_type=jnp.float32)
        u = jnp.dot(recvd[...], buf[j, 1], preferred_element_type=jnp.float32)
        return g / (1.0 + jnp.exp(-g)) * u

    def own_block(j):
        own_hid[j] = gated(own, j).astype(jnp.bfloat16)

    def other_block(j):
        h = gated(oth, j)
        rows = lax.broadcasted_iota(jnp.int32, h.shape, 0)
        mix = jnp.where((rows & (ROWS - 1)) < ROWS // 2, own_hid[j].astype(jnp.float32), h)
        hid[j] = mix.astype(jnp.bfloat16)

    first = jnp.where(d == 0, 0, NJ - 1)
    second = NJ - 1 - first
    n2 = NB + 2 + jnp.maximum((last - 2 * k) * HOP + 6, 0)
    lag = jnp.where(k == last, LAG, 0)
    bound = jnp.maximum(count(k), n2 + 1)

    def mate_wait(s, _):
        cp(rel, oth, theirs(s), x_s, recv_d, mid).wait_recv()
        return 0

    def body(n, _):
        o = n + LEAD
        pl.when((k == 0) & (o < wopp))(lambda: opp_send(o).start())
        pl.when((k == last) & (n < count(0)))(lambda: first_send(n).wait_send())
        pl.when((k == last) & (o < count(0)))(lambda: first_send(o).start())
        s = n - lag

        @pl.when((s >= 0) & (s < count(k)))
        def _():
            c = mine(s)
            onward = (k < last) & (s < count(k + 1))
            direct = cp(oth, oth, c, fwd_d, recv_d, nxt)
            relayed = cp(rel, rel, c, fwd_r, recv_r, nxt)
            direct.wait_recv()
            pl.when(onward)(lambda: direct.start())
            relayed.wait_recv()
            pl.when(onward)(lambda: relayed.start())
            cp(rel, oth, c, x_s, recv_d, mid).start()

        pl.when(s >= 0)(lambda: deltas(s))
        pl.when((k < 8) & (n < PLANE - 1))(lambda: dispatch(n))

        @pl.when(s == NB - 3)
        def _():
            pltpu.make_async_copy(recvd.at[pl.ds(0, (PLANE - 1) * ROWS)], recvd.at[pl.ds(0, (PLANE - 1) * ROWS)], disp_r).wait()
            own_rows.wait()

        pl.when((s >= NB - 3) & (s < NB - 3 + NJ))(lambda: own_block(s - NB + 3))
        pl.when(s == NB)(lambda: other_block(first))

        @pl.when(s == n2)
        def _():
            lax.fori_loop(0, NB, mate_wait, 0)
            other_block(second)

        return 0

    lax.fori_loop(0, bound + lag, body, 0)
    lax.fori_loop(NB, M - count(k), mate_wait, 0)
    for j in range(1, NJ - 1):
        other_block(j)

    def give_back(n, _):
        q, dev = peer(n)
        pltpu.make_async_remote_copy(src_ref=hid.at[:, block(q)], dst_ref=ret.at[:, block(me)], send_sem=ret_s,
                                     recv_sem=ret_r, device_id=dev, device_id_type=MESH).start()
        return 0

    lax.fori_loop(0, PLANE - 1, give_back, 0)
    keep = pltpu.make_async_copy(hid.at[:, block(me)], ret.at[:, block(me)], loc_s.at[1])
    keep.start()

    def fin(s, _):
        c = mine(s)

        @pl.when((k < last) & (s < count(k + 1)))
        def _():
            cp(oth, oth, c, fwd_d, recv_d, nxt).wait_send()
            cp(rel, rel, c, fwd_r, recv_r, nxt).wait_send()

        pl.when(s < count(k))(lambda: cp(rel, oth, c, x_s, recv_d, mid).wait_send())
        pl.when((k == 0) & (s < wopp))(lambda: opp_send(s).wait_send())
        return 0

    lax.fori_loop(0, M // 2 + 2 * SHIFT + 1, fin, 0)
    pltpu.make_async_copy(outg.at[pl.ds(0, (PLANE - 1) * ROWS)], outg.at[pl.ds(0, (PLANE - 1) * ROWS)], disp_s).wait()
    for c in range(PIECES):
        pl.when((k != CEN) & (k != CEN + 1))(lambda: pcopy(acc, part, c, in_s, in_r, nxt).wait_send())
        pl.when((k == CEN) | (k == CEN + 1))(lambda: pcopy(acc, xin, c, xin_s, xin_r, nxt).wait_send())
        pl.when((k > 0) & (k < last))(lambda: pcopy(total, total, c, tot_s, tot_r, nxt).wait_send())

    others = pl.ds(0, (PLANE - 1) * ROWS)
    pltpu.make_async_copy(ret.at[:, others], ret.at[:, others], ret_r).wait()
    keep.wait()
    for t in range(2):
        for j in range(NJ):
            got = jnp.dot(pick[t], ret[j], preferred_element_type=jnp.float32)
            mixed[t, :, pl.ds(j * CB, CB)] = (weights[:, t:t + 1] * got).astype(jnp.bfloat16)
    pltpu.make_async_copy(hid.at[:, others], hid.at[:, others], ret_s).wait()


def shards(tokens, routes, route_weight, gate_weight, up_weight, local_params, base, momentum):
    frag, cols = base.shape
    wide = cols // PIECES
    bf, f32 = jnp.bfloat16, jnp.float32
    vmem = pl.BlockSpec(memory_space=pltpu.VMEM)
    hbm = pl.BlockSpec(memory_space=pl.ANY)
    sems = pltpu.SemaphoreType.DMA
    mixed, total = pl.pallas_call(
        kernel,
        out_shape=(jax.ShapeDtypeStruct((2, TOK, HW), bf), jax.ShapeDtypeStruct((PIECES, frag, wide), f32)),
        in_specs=[vmem, vmem, vmem, hbm, hbm, vmem, vmem],
        out_specs=(vmem, vmem),
        scratch_shapes=[
            pltpu.VMEM((NJ, 2, DW, CB), bf), pltpu.VMEM((NJ, 2, DW, CB), bf), pltpu.VMEM((NJ, 2, DW, CB), bf),
            pltpu.VMEM((PLANE * ROWS, DW), bf), pltpu.VMEM((PLANE * ROWS, DW), bf),
            pltpu.VMEM((NJ, PLANE * ROWS, CB), bf), pltpu.VMEM((NJ, PLANE * ROWS, CB), bf),
            pltpu.VMEM((NJ, PLANE * ROWS, CB), bf), pltpu.VMEM((2, TOK, PLANE * ROWS), bf),
            pltpu.VMEM((PIECES, frag, wide), f32), pltpu.VMEM((PIECES, frag, wide), f32), pltpu.VMEM((PIECES, frag, wide), f32),
            sems((NJ, 2)), sems((M,)), sems((M,)), sems((M,)), sems((M,)), sems((M,)), sems((M,)),
            sems, sems, sems, sems, sems((2,)),
            sems((PIECES,)), sems((PIECES,)), sems((PIECES,)), sems((PIECES,)), sems((PIECES,)), sems((PIECES,)),
        ],
        compiler_params=pltpu.CompilerParams(collective_id=0, has_side_effects=True, vmem_limit_bytes=56 << 20),
        cost_estimate=pl.CostEstimate(flops=8 * PLANE * ROWS * DW * HW, bytes_accessed=10 << 20, transcendentals=0),
    )(tokens[0], routes[0], route_weight[0], gate_weight[0], up_weight[0], local_params[0], base)
    mixed = mixed.transpose(1, 0, 2)[None]
    outer_grad = total.transpose(1, 0, 2).reshape(frag, cols) / LINE
    new_momentum = outer_beta * momentum + outer_grad
    new_base = base - outer_rate * (outer_grad + outer_beta * new_momentum)
    return (mixed, new_base, new_momentum)


def solution(mesh):
    in_specs = (
        P("replica", "expert", None),
        P("replica", "expert", None),
        P("replica", "expert", None),
        P("expert", None, None),
        P("expert", None, None),
        P("replica", "expert", None),
        P("expert", None),
        P("expert", None),
    )
    out_specs = (P("replica", "expert", None, None), P("expert", None), P("expert", None))
    return jax.shard_map(shards, mesh=mesh, in_specs=in_specs, out_specs=out_specs, check_vma=False)
```

time: 520 us -> 181 us (0.35)
  blocking collectives: 460 us -> 0 us
  Pallas kernels: 0 us -> 173 us
  starting transfers between devices: 39 us -> 0 us
  matrix products: 8.11 us -> 0 us
    psum x1 -> x0, blocking collectives: 328 us -> none  [shards(): outer_grad = lax.psum(delta, 'replica') / n_replica]
    pallas_call x0 -> x1, Pallas kernels: none -> 173 us  [shards(): pl.pallas_call(kernel, out_shape=(jax.ShapeDtypeStruct((2, TOK, HW), bf),...]
    all_to_all x1 -> x0, blocking collectives: 132 us -> none  [shards(): lax.all_to_all(outgoing, 'expert', split_axis=0, concat_axis=0, tiled=True)]
    all_to_all x1 -> x0, starting transfers between devices: 39 us -> none  [shards(): lax.all_to_all((jax.nn.silu(gate) * upper).astype(jnp.bfloat16).reshape(s...]
    dot_general x4 -> x0, matrix products: 8.11 us -> none  [the longest x1 3.94 us: shards(): gate = jnp.dot(flat, w_gate, preferred_element_type=jnp.float32)]
    reshape x5 -> x0, local copies, waits for them, and re-layouts: 7.54 us -> none  [the longest x1 2.76 us: shards(): flat = received.reshape(sources * slots, width)]
  transfers between devices with their start and end apart: 1 -> 0, of which waited for: 0 -> 0; matrix products, arithmetic and copies ran while one was open for 0% -> 0% of each run, Pallas kernels for 0% -> 0%
where the time goes in v1:
time: 181 us; the launch traced here: 180 us
  Pallas kernels  173 us (96%)
  local copies, waits for them, and re-layouts  5 us (3%)
  other arithmetic  1.83 us (1%)
    pallas_call x1, Pallas kernels, shards(): pl.pallas_call(kernel, out_shape=(jax.ShapeDtypeStruct((2, TOK, HW), bf),...  173 us
    unnamed x7, local copies, waits for them, and re-layouts  4.98 us

profile of v1, /device:TPU:6, one launch (start us, length us, event | category | flops | bytes accessed | tf_op | source)
XLA Modules:
  0.0 180.1 jit_solution(11495032871734186)
XLA Ops:
  0.6 1.4 copy.14
  2.0 1.4 copy.15
  3.5 0.0 copy-start
  3.5 0.0 copy-start.1
  3.5 172.7 %shard_map.103 = (bf16[2,128,768]{2,1,0:T(8,128)(2,1)}, f32[4,32,512]{2,1,0:T(8,128)}) custom-call(bf16[128,2560]{1,0:T(8,128)(2,1)} %bitcast.19, s32[128,2]{1,0:T(8,128)} %bitcast.15, f32[128,2]{1,0:T(8,128)} %bitcast.16, bf16[2560,768]{1,0:T(8,128)(2,1)} %bitcast.17, bf16[2560,768]{1,0:T(8,128)(2,1)} %bitcast.18, bf16[32,2048]{1,0:T(8,128)(2,1)} %bitcast.20, ...), custom_call_target="tpu_custom_call" | custom-call | flops 8053063680 | bytes 10485760 | tf_op jit(solution)/shard_map/pallas_call | solution.py:317
  176.1 2.1 %copy.17 = bf16[1,128,2,768]{3,2,1,0:T(2,128)(2,1)} copy(bf16[1,128,2,768]{3,1,2,0:T(8,128)(2,1)} %bitcast.14) | data formatting | bytes 786432
  178.3 1.0 multiply_bitcast_fusion
  179.3 0.0 copy-done
  179.3 0.0 copy-done.1
  179.3 0.9 multiply_subtract_fusion
  (1 shorter events, 0.0 us)
Async XLA Ops:
  3.5 175.8 %copy-start = (f32[32,2048]{1,0:T(8,128)S(1)}, f32[32,2048]{1,0:T(8,128)}, u32[]{:S(2)}) copy-start(f32[32,2048]{1,0:T(8,128)} %base.1) | copy-start | bytes 786436
  3.5 175.8 %copy-start.1 = (f32[32,2048]{1,0:T(8,128)S(1)}, f32[32,2048]{1,0:T(8,128)}, u32[]{:S(2)}) copy-start(f32[32,2048]{1,0:T(8,128)} %param.15) | copy-start | bytes 786436

commit v2 on v1

--- a/solution.py
+++ b/solution.py
@@ -19,12 +19,13 @@
 NR = DW // CHUNK
 NB = 2 * NR
 M = NJ * NB
-SHIFT = 8
+SHIFT = 10
 LEAD = 6
-LAG = 45
+LAG = 50
 PIECES = 4
 CEN = 8
 HOP = 3
+DRAIN = 8
 
 
 def received(a):
@@ -32,7 +33,7 @@
 
 
 def kernel(tok, routes, weights, gate_hbm, up_hbm, local, base, mixed, total,
-           own, oth, rel, outg, recvd, own_hid, hid, ret, pick, part, acc, xin,
+           own, oth, rel, outg, recvd, rows_own, rows_oth, own_hid, hid, ret, pick, wide, part, acc, xin,
            load_sem, recv_d, recv_r, fwd_d, fwd_r, x_s, own_r,
            disp_s, disp_r, ret_s, ret_r, loc_s, in_r, in_s, xin_r, xin_s, tot_r, tot_s):
     i = lax.axis_index("replica")
@@ -72,7 +73,7 @@
         pl.semaphore_signal(barrier, inc=1, device_id=opp, device_id_type=MESH)
 
     loads = []
-    for j in (0, *range(NJ - 1, 0, -1)):
+    for j in (0, NJ - 1, *range(1, NJ - 1)):
         for g, ref in enumerate((gate_hbm, up_hbm)):
             loads.append(pltpu.make_async_copy(ref.at[:, pl.ds(j * CB, CB)], own.at[j, g], load_sem.at[j, g]))
     for copy in loads:
@@ -84,7 +85,7 @@
 
     lax.fori_loop(0, PLANE - 1, greet, 0)
     pl.semaphore_wait(barrier, PLANE + 1 + jnp.where(k == 0, 1, 0))
-    for copy in loads:
+    for copy in loads[:4]:
         copy.wait()
 
     def at(buf, c):
@@ -114,20 +115,22 @@
 
     lax.fori_loop(0, LEAD, lead_body, 0)
 
-    lanes = lax.broadcasted_iota(jnp.int32, (TOK, 2 * PLANE), 1)
-    r = [routes[:, 0:1], routes[:, 1:2]]
-    named = ((r[0] == lanes) | (r[1] == lanes)).astype(jnp.float32)
-    before = (lax.broadcasted_iota(jnp.int32, (TOK, TOK), 1) < lax.broadcasted_iota(jnp.int32, (TOK, TOK), 0))
-    ranks = jnp.dot(before.astype(jnp.bfloat16), named.astype(jnp.bfloat16), preferred_element_type=jnp.float32)
-    slots = lax.broadcasted_iota(jnp.int32, (TOK, PLANE * ROWS), 1)
-    place = jnp.zeros((TOK, PLANE * ROWS), jnp.float32)
+    names = lax.broadcasted_iota(jnp.int32, (2 * PLANE, TOK), 0)
+    r = [routes[0:1, :], routes[1:2, :]]
+    named = ((r[0] == names) | (r[1] == names)).astype(jnp.float32)
+    before = (lax.broadcasted_iota(jnp.int32, (TOK, TOK), 0) < lax.broadcasted_iota(jnp.int32, (TOK, TOK), 1))
+    before = before.astype(jnp.float32)
+    ranks = jnp.dot(named.astype(jnp.bfloat16), before.astype(jnp.bfloat16), preferred_element_type=jnp.float32)
+    slots = lax.broadcasted_iota(jnp.int32, (PLANE * ROWS, TOK), 0)
+    place = jnp.zeros((PLANE * ROWS, TOK), jnp.float32)
     for t in range(2):
-        rank = jnp.sum(jnp.where(r[t] == lanes, ranks, 0.0), axis=1, keepdims=True).astype(jnp.int32)
+        rank = jnp.sum(jnp.where(r[t] == names, ranks, 0.0), axis=0, keepdims=True).astype(jnp.int32)
         row = (r[t] & (PLANE - 1)) * ROWS + jnp.where(r[t] // PLANE == half, 0, ROWS // 2) + rank
         one = (row == slots).astype(jnp.float32)
-        pick[t] = one.astype(jnp.bfloat16)
+        pick[t] = one.T.astype(jnp.bfloat16)
+        wide[t] = jnp.broadcast_to(weights[t:t + 1, :], (TOK, TOK)).T
         place += one
-    place_t = place.T.astype(jnp.bfloat16)
+    place_t = place.astype(jnp.bfloat16)
     for c in range(DW // 512):
         cols = pl.ds(c * 512, 512)
         outg[:, cols] = jnp.dot(place_t, tok[:, cols], preferred_element_type=jnp.float32).astype(jnp.bfloat16)
@@ -150,16 +153,12 @@
             return 0
         lax.fori_loop(0, PLANE - 1, body, 0)
 
-    width = part.shape[2]
-
     def pcopy(src, dst, c, ss, rs, dev):
         return pltpu.make_async_remote_copy(src_ref=src.at[c], dst_ref=dst.at[c], send_sem=ss.at[c],
                                             recv_sem=rs.at[c], device_id=dev, device_id_type=MESH)
 
-    for c in range(PIECES):
-        cols = pl.ds(c * width, width)
-        delta = (base[:, cols] - local[:, cols].astype(jnp.float32)).astype(jnp.bfloat16)
-        acc[c] = delta.astype(jnp.float32)
+    delta = (base[...] - local[...].astype(jnp.float32)).astype(jnp.bfloat16).astype(jnp.float32)
+    acc[...] = delta.reshape(acc.shape)
 
     @pl.when(k > CEN)
     def _():
@@ -202,29 +201,61 @@
             pl.when((k < CEN) & (k > 0))(lambda: pcopy(total, total, back, tot_s, tot_r, prv).start())
             pl.when((k > CEN + 1) & (k < last))(lambda: pcopy(total, total, back, tot_s, tot_r, nxt).start())
 
-    def gated(buf, j):
-        g = jnp.dot(recvd[...], buf[j, 0], preferred_element_type=jnp.float32)
-        u = jnp.dot(recvd[...], buf[j, 1], preferred_element_type=jnp.float32)
+    def split():
+        for c in range(DW // 512):
+            cols = pl.ds(c * 512, 512)
+            both = recvd[:, cols].astype(jnp.float32).reshape(PLANE, ROWS, 512)
+            rows_own[:, cols] = both[:, :ROWS // 2].reshape(PLANE * ROWS // 2, 512).astype(jnp.bfloat16)
+            rows_oth[:, cols] = both[:, ROWS // 2:].reshape(PLANE * ROWS // 2, 512).astype(jnp.bfloat16)
+
+    def gated(rows, buf, j):
+        g = jnp.dot(rows[...], buf[j, 0], preferred_element_type=jnp.float32)
+        u = jnp.dot(rows[...], buf[j, 1], preferred_element_type=jnp.float32)
         return g / (1.0 + jnp.exp(-g)) * u
 
     def own_block(j):
-        own_hid[j] = gated(own, j).astype(jnp.bfloat16)
+        own_hid[j] = gated(rows_own, own, j)
 
     def other_block(j):
-        h = gated(oth, j)
-        rows = lax.broadcasted_iota(jnp.int32, h.shape, 0)
-        mix = jnp.where((rows & (ROWS - 1)) < ROWS // 2, own_hid[j].astype(jnp.float32), h)
-        hid[j] = mix.astype(jnp.bfloat16)
+        h = gated(rows_oth, oth, j).reshape(PLANE, ROWS // 2, CB)
+        both = jnp.concatenate([own_hid[j].reshape(PLANE, ROWS // 2, CB), h], axis=1)
+        hid[j] = both.reshape(PLANE * ROWS, CB).astype(jnp.bfloat16)
+
+    def give_back(n, j):
+        q, dev = peer(n)
+        pltpu.make_async_remote_copy(src_ref=hid.at[j, block(q)], dst_ref=ret.at[j, block(me)], send_sem=ret_s.at[j],
+                                     recv_sem=ret_r.at[j], device_id=dev, device_id_type=MESH).start()
+
+    def keep(j):
+        return pltpu.make_async_copy(hid.at[j, block(me)], ret.at[j, block(me)], loc_s.at[1 + j])
+
+    def give_all(j, begin):
+        def body(n, _):
+            give_back(n, j)
+            return 0
+        lax.fori_loop(begin, PLANE - 1, body, 0)
+        keep(j).start()
 
     first = jnp.where(d == 0, 0, NJ - 1)
     second = NJ - 1 - first
     n2 = NB + 2 + jnp.maximum((last - 2 * k) * HOP + 6, 0)
     lag = jnp.where(k == last, LAG, 0)
     bound = jnp.maximum(count(k), n2 + 1)
+    loads[4].wait()
+    loads[5].wait()
 
     def mate_wait(s, _):
         cp(rel, oth, theirs(s), x_s, recv_d, mid).wait_recv()
         return 0
+
+    def drain(s):
+        c = mine(s)
+        cp(rel, oth, c, x_s, recv_d, mid).wait_send()
+
+        @pl.when((k < last) & (s < count(k + 1)))
+        def _():
+            cp(oth, oth, c, fwd_d, recv_d, nxt).wait_send()
+            cp(rel, rel, c, fwd_r, recv_r, nxt).wait_send()
 
     def body(n, _):
         o = n + LEAD
@@ -244,53 +275,40 @@
             relayed.wait_recv()
             pl.when(onward)(lambda: relayed.start())
             cp(rel, oth, c, x_s, recv_d, mid).start()
-
+            pl.when(s >= DRAIN)(lambda: drain(s - DRAIN))
+
+        pl.when((k == 0) & (n >= DRAIN) & (n < wopp))(lambda: opp_send(n - DRAIN).wait_send())
         pl.when(s >= 0)(lambda: deltas(s))
         pl.when((k < 8) & (n < PLANE - 1))(lambda: dispatch(n))
 
-        @pl.when(s == NB - 3)
+        @pl.when(s == NB - 4)
         def _():
             pltpu.make_async_copy(recvd.at[pl.ds(0, (PLANE - 1) * ROWS)], recvd.at[pl.ds(0, (PLANE - 1) * ROWS)], disp_r).wait()
             own_rows.wait()
+            split()
 
         pl.when((s >= NB - 3) & (s < NB - 3 + NJ))(lambda: own_block(s - NB + 3))
         pl.when(s == NB)(lambda: other_block(first))
+        pl.when((s > NB) & (s < NB + PLANE))(lambda: give_back(s - NB - 1, first))
 
         @pl.when(s == n2)
         def _():
             lax.fori_loop(0, NB, mate_wait, 0)
             other_block(second)
+            give_all(second, 0)
 
         return 0
 
     lax.fori_loop(0, bound + lag, body, 0)
+    give_all(first, jnp.minimum(bound - NB - 1, PLANE - 1))
     lax.fori_loop(NB, M - count(k), mate_wait, 0)
     for j in range(1, NJ - 1):
         other_block(j)
-
-    def give_back(n, _):
-        q, dev = peer(n)
-        pltpu.make_async_remote_copy(src_ref=hid.at[:, block(q)], dst_ref=ret.at[:, block(me)], send_sem=ret_s,
-                                     recv_sem=ret_r, device_id=dev, device_id_type=MESH).start()
-        return 0
-
-    lax.fori_loop(0, PLANE - 1, give_back, 0)
-    keep = pltpu.make_async_copy(hid.at[:, block(me)], ret.at[:, block(me)], loc_s.at[1])
-    keep.start()
-
-    def fin(s, _):
-        c = mine(s)
-
-        @pl.when((k < last) & (s < count(k + 1)))
-        def _():
-            cp(oth, oth, c, fwd_d, recv_d, nxt).wait_send()
-            cp(rel, rel, c, fwd_r, recv_r, nxt).wait_send()
-
-        pl.when(s < count(k))(lambda: cp(rel, oth, c, x_s, recv_d, mid).wait_send())
-        pl.when((k == 0) & (s < wopp))(lambda: opp_send(s).wait_send())
-        return 0
-
-    lax.fori_loop(0, M // 2 + 2 * SHIFT + 1, fin, 0)
+        give_all(j, 0)
+
+    for n in range(DRAIN):
+        drain(count(k) - DRAIN + n)
+        pl.when(k == 0)(lambda: opp_send(wopp - DRAIN + n).wait_send())
     pltpu.make_async_copy(outg.at[pl.ds(0, (PLANE - 1) * ROWS)], outg.at[pl.ds(0, (PLANE - 1) * ROWS)], disp_s).wait()
     for c in range(PIECES):
         pl.when((k != CEN) & (k != CEN + 1))(lambda: pcopy(acc, part, c, in_s, in_r, nxt).wait_send())
@@ -298,42 +316,49 @@
         pl.when((k > 0) & (k < last))(lambda: pcopy(total, total, c, tot_s, tot_r, nxt).wait_send())
 
     others = pl.ds(0, (PLANE - 1) * ROWS)
-    pltpu.make_async_copy(ret.at[:, others], ret.at[:, others], ret_r).wait()
-    keep.wait()
-    for t in range(2):
-        for j in range(NJ):
+
+    def combine(j):
+        pltpu.make_async_copy(ret.at[j, others], ret.at[j, others], ret_r.at[j]).wait()
+        keep(j).wait()
+        for t in range(2):
             got = jnp.dot(pick[t], ret[j], preferred_element_type=jnp.float32)
-            mixed[t, :, pl.ds(j * CB, CB)] = (weights[:, t:t + 1] * got).astype(jnp.bfloat16)
-    pltpu.make_async_copy(hid.at[:, others], hid.at[:, others], ret_s).wait()
+            mixed[t, :, pl.ds(pl.multiple_of(j * CB, CB), CB)] = (wide[t][:, 0:1] * got).astype(jnp.bfloat16)
+
+    combine(first)
+    combine(second)
+    for j in range(1, NJ - 1):
+        combine(j)
+    for j in range(NJ):
+        pltpu.make_async_copy(hid.at[j, others], hid.at[j, others], ret_s.at[j]).wait()
 
 
 def shards(tokens, routes, route_weight, gate_weight, up_weight, local_params, base, momentum):
     frag, cols = base.shape
-    wide = cols // PIECES
     bf, f32 = jnp.bfloat16, jnp.float32
     vmem = pl.BlockSpec(memory_space=pltpu.VMEM)
     hbm = pl.BlockSpec(memory_space=pl.ANY)
     sems = pltpu.SemaphoreType.DMA
     mixed, total = pl.pallas_call(
         kernel,
-        out_shape=(jax.ShapeDtypeStruct((2, TOK, HW), bf), jax.ShapeDtypeStruct((PIECES, frag, wide), f32)),
+        out_shape=(jax.ShapeDtypeStruct((2, TOK, HW), bf), jax.ShapeDtypeStruct((PIECES, frag // PIECES, cols), f32)),
         in_specs=[vmem, vmem, vmem, hbm, hbm, vmem, vmem],
         out_specs=(vmem, vmem),
         scratch_shapes=[
             pltpu.VMEM((NJ, 2, DW, CB), bf), pltpu.VMEM((NJ, 2, DW, CB), bf), pltpu.VMEM((NJ, 2, DW, CB), bf),
             pltpu.VMEM((PLANE * ROWS, DW), bf), pltpu.VMEM((PLANE * ROWS, DW), bf),
-            pltpu.VMEM((NJ, PLANE * ROWS, CB), bf), pltpu.VMEM((NJ, PLANE * ROWS, CB), bf),
-            pltpu.VMEM((NJ, PLANE * ROWS, CB), bf), pltpu.VMEM((2, TOK, PLANE * ROWS), bf),
-            pltpu.VMEM((PIECES, frag, wide), f32), pltpu.VMEM((PIECES, frag, wide), f32), pltpu.VMEM((PIECES, frag, wide), f32),
+            pltpu.VMEM((PLANE * ROWS // 2, DW), bf), pltpu.VMEM((PLANE * ROWS // 2, DW), bf),
+            pltpu.VMEM((NJ, PLANE * ROWS // 2, CB), f32), pltpu.VMEM((NJ, PLANE * ROWS, CB), bf),
+            pltpu.VMEM((NJ, PLANE * ROWS, CB), bf), pltpu.VMEM((2, TOK, PLANE * ROWS), bf), pltpu.VMEM((2, TOK, TOK), f32),
+            pltpu.VMEM((PIECES, frag // PIECES, cols), f32), pltpu.VMEM((PIECES, frag // PIECES, cols), f32), pltpu.VMEM((PIECES, frag // PIECES, cols), f32),
             sems((NJ, 2)), sems((M,)), sems((M,)), sems((M,)), sems((M,)), sems((M,)), sems((M,)),
-            sems, sems, sems, sems, sems((2,)),
+            sems, sems, sems((NJ,)), sems((NJ,)), sems((1 + NJ,)),
             sems((PIECES,)), sems((PIECES,)), sems((PIECES,)), sems((PIECES,)), sems((PIECES,)), sems((PIECES,)),
         ],
         compiler_params=pltpu.CompilerParams(collective_id=0, has_side_effects=True, vmem_limit_bytes=56 << 20),
         cost_estimate=pl.CostEstimate(flops=8 * PLANE * ROWS * DW * HW, bytes_accessed=10 << 20, transcendentals=0),
-    )(tokens[0], routes[0], route_weight[0], gate_weight[0], up_weight[0], local_params[0], base)
+    )(tokens[0], routes[0].T, route_weight[0].T, gate_weight[0], up_weight[0], local_params[0], base)
     mixed = mixed.transpose(1, 0, 2)[None]
-    outer_grad = total.transpose(1, 0, 2).reshape(frag, cols) / LINE
+    outer_grad = total.reshape(frag, cols) / LINE
     new_momentum = outer_beta * momentum + outer_grad
     new_base = base - outer_rate * (outer_grad + outer_beta * new_momentum)
     return (mixed, new_base, new_momentum)

time: 181 us -> 170 us (0.939)
  Pallas kernels: 173 us -> 163 us
  local copies, waits for them, and re-layouts: 5 us -> 2.16 us
    pallas_call x1, Pallas kernels: 173 us -> 163 us  [shards(): pl.pallas_call(kernel, out_shape=(jax.ShapeDtypeStruct((2, TOK, HW), bf),...]
    unnamed x7 -> x5, local copies, waits for them, and re-layouts: 4.98 us -> 2.16 us
where the time goes in v2:
time: 170 us; the launch traced here: 168 us
  Pallas kernels  163 us (96%)
  local copies, waits for them, and re-layouts  2.16 us (1%)
  other arithmetic  1.81 us (1%)
    pallas_call x1, Pallas kernels, shards(): pl.pallas_call(kernel, out_shape=(jax.ShapeDtypeStruct((2, TOK, HW), bf),...  163 us

profile of v2, /device:TPU:6, one launch (start us, length us, event | category | flops | bytes accessed | tf_op | source)
XLA Modules:
  0.0 167.7 jit_solution(494858259928349905)
XLA Ops:
  0.6 0.0 copy-start
  0.6 0.0 copy-start.1
  0.7 163.1 %shard_map.103 = (bf16[2,128,768]{2,1,0:T(8,128)(2,1)}, f32[4,8,2048]{2,1,0:T(8,128)}) custom-call(bf16[128,2560]{1,0:T(8,128)(2,1)} %bitcast.24, s32[2,128]{1,0:T(2,128)} %bitcast.26, f32[2,128]{1,0:T(2,128)} %bitcast.27, bf16[2560,768]{1,0:T(8,128)(2,1)} %bitcast.22, bf16[2560,768]{1,0:T(8,128)(2,1)} %bitcast.23, bf16[32,2048]{1,0:T(8,128)(2,1)} %bitcast.25, ...), custom_call_target="tpu_custom_call" | custom-call | flops 8053063680 | bytes 10485760 | tf_op jit(solution)/shard_map/pallas_call | solution.py:341
  163.7 2.1 %copy.11 = bf16[1,128,2,768]{3,2,1,0:T(2,128)(2,1)} copy(bf16[1,128,2,768]{3,1,2,0:T(8,128)(2,1)} %bitcast.21) | data formatting | bytes 786432
  165.9 0.0 copy-done
  165.9 0.0 copy-done.1
  165.9 1.8 %fusion.1 = (f32[32,2048]{1,0:T(8,128)}, f32[32,2048]{1,0:T(8,128)}) fusion(f32[32,2048]{1,0:T(8,128)S(1)} %copy-done, f32[4,8,2048]{2,1,0:T(8,128)} %get-tuple-element.6, f32[32,2048]{1,0:T(8,128)S(1)} %copy-done.1), kind=kLoop, calls=%fused_computation.3 | loop fusion | flops 458752 | bytes 1310720 | tf_op jit(solution)/shard_map/sub | solution.py:363
Async XLA Ops:
  0.6 165.2 %copy-start = (f32[32,2048]{1,0:T(8,128)S(1)}, f32[32,2048]{1,0:T(8,128)}, u32[]{:S(2)}) copy-start(f32[32,2048]{1,0:T(8,128)} %base.1) | copy-start | bytes 786436
  0.6 165.2 %copy-start.1 = (f32[32,2048]{1,0:T(8,128)S(1)}, f32[32,2048]{1,0:T(8,128)}, u32[]{:S(2)}) copy-start(f32[32,2048]{1,0:T(8,128)} %param.15) | copy-start | bytes 786436
